TPU v7x, 32 devices: a whole 2x2x4 slice. The times are simulated.
32 devices in a mesh: ctx: 16 (over z, y, core), head: 2 (over x).
Axes of the slice: x: 2, y: 2, z: 4, core: 2. Of those that a mesh axis runs over, the one named last changes fastest.
Arguments:
- queries: bfloat16 [2048, 5120], P('ctx', 'head'), may hold values from -80 to 80
- keys: bfloat16 [2048, 1024], P('ctx', 'head'), may hold values from -4 to 4
- values: bfloat16 [2048, 1024], P('ctx', 'head'), may hold values from -6 to 6
- out_grad: bfloat16 [2048, 5120], P('ctx', 'head'), may hold values from -6 to 6
- out_weight: bfloat16 [5120, 5120], P('head'), may hold values from -0.078125 to 0.078125
- seq_lengths: int32 [4], replicated, may hold values from 1 to 1024, as said below
- prompt_lengths: int32 [4], replicated, may hold values from 1 to 127
Outputs:
- query_grad: bfloat16 [2048, 5120], P('ctx', 'head')
- key_grad: bfloat16 [2048, 1024], P('ctx', 'head')
- value_grad: bfloat16 [2048, 1024], P('ctx', 'head')
Inputs may be any that keep to these rules, and one draw needn't show every extreme that they name: `seq_lengths`: the lengths sum to 2048; the first is exactly 1024.
All inputs are finite; a program needn't handle non-finite values.
Results may differ from a plain program's by a relative error of at most 0.015.
Values may be sent and summed in bfloat16 or wider, within the bound.
A program may use at most 64 MiB of HBM per device.

v0:
```python
import functools
import math

import jax
import jax.numpy as jnp
from jax import lax
from jax.experimental import pallas as pl
from jax.experimental.pallas import tpu as pltpu
from jax.sharding import PartitionSpec as P

HEADS_Q = 40
HEADS_KV = 8
HEAD_DIM = 128
GROUP = HEADS_Q // HEADS_KV
SCALE = 1.0 / math.sqrt(HEAD_DIM)
NEG_LARGE = -1e30
NT = (((1,), (1,)), ((), ()))
NN = (((1,), (0,)), ((), ()))
TN = (((0,), (0,)), ((), ()))


def dot(a, b, dims):
    return lax.dot_general(a, b, dims, preferred_element_type=jnp.float32)


def segment_facts(seq_ref, prompt_ref, positions):
    start = jnp.zeros_like(positions)
    first = jnp.zeros_like(positions)
    begin = 0
    for s in range(seq_ref.shape[0]):
        length = seq_ref[s]
        reached = positions >= begin
        start = jnp.where(reached, begin, start)
        first = jnp.where(reached, begin + jnp.minimum(prompt_ref[s], length - 1), first)
        begin = begin + length
    return start, first


def kernel(
    nctx, nhead, chunk,
    q_ref, k_ref, v_ref, og_ref, w_ref, seq_ref, prompt_ref,
    dq_ref, dk_ref, dv_ref,
    wbuf, ogbuf, acc, qs, gs, kbuf, vbuf, probs, peaks, top_ref, mass, dprobs, dqt, part, sib, total, sums, ret,
    w_sem, og_send, og_recv, k_send, v_send, k_recv, v_recv, k_fwd, v_fwd,
    sib_send, sib_recv, ret_send, ret_recv,
):
    count = q_ref.shape[0]
    kv_local = k_ref.shape[1] // HEAD_DIM
    chips = nctx // 4
    features = w_ref.shape[0]
    part_width = og_ref.shape[1]
    chunks = part_width // chunk
    me = lax.axis_index("ctx")
    head = lax.axis_index("head")
    half = me // (nctx // 2)
    base = half * (nctx // 2)
    core = me % 2
    other = 1 - core
    chip = (me - base) // 2
    sibling = me + 1 - 2 * core

    def remote(src, dst, send, recv, ctx, head_at):
        return pltpu.make_async_remote_copy(
            src_ref=src, dst_ref=dst, send_sem=send, recv_sem=recv,
            device_id=(ctx, head_at), device_id_type=pl.DeviceIdType.MESH,
        )

    def same_core(p):
        return base + 2 * p + core

    def w_copy(t):
        column = ((head + t // chunks) % nhead) * part_width + (t % chunks) * chunk
        return pltpu.make_async_copy(
            w_ref.at[:, pl.ds(pl.multiple_of(column, 128), chunk)], wbuf.at[t], w_sem.at[t]
        )

    for t in range(nhead * chunks):
        w_copy(t).start()

    barrier = pltpu.get_barrier_semaphore()

    def greet(ctx, head_at):
        pl.semaphore_signal(
            barrier, inc=1, device_id=(ctx, head_at), device_id_type=pl.DeviceIdType.MESH
        )

    for o in range(1, nhead):
        greet(me, (head + o) % nhead)
    greet(sibling, head)
    for o in range(1, chips):
        greet(same_core((chip + o) % chips), head)
    pl.semaphore_wait(barrier, nhead - 1 + 1 + chips - 1)

    def og_copy(o, ch):
        return remote(
            og_ref.at[:, pl.ds(ch * chunk, chunk)], ogbuf.at[o - 1, ch],
            og_send.at[o - 1, ch], og_recv.at[o - 1, ch], me, (head + nhead - o) % nhead,
        )

    for ch in range(chunks):
        for o in range(1, nhead):
            og_copy(o, ch).start()

    def direct(ref, buf, send, recv, p):
        return remote(ref, buf.at[chip, core], send.at[p], recv.at[chip, core], same_core(p), head)

    def to_sibling(ref, buf, send, recv, p):
        return remote(ref, buf.at[p, core], send.at[p], recv.at[p, core], sibling, head)

    def arrived(ref, buf, recv, p, c):
        pltpu.make_async_copy(ref, buf.at[p, c], recv.at[p, c]).wait()

    pairs = ((k_ref, kbuf, k_send, k_recv, k_fwd), (v_ref, vbuf, v_send, v_recv, v_fwd))
    def push(ref, buf, send, recv, fwd):
        to_sibling(ref, buf, fwd, recv, chip).start()

        def send_direct(p, carry):
            direct(ref, buf, send, recv, p).start()
            return carry

        lax.fori_loop(chip + 1, chips, send_direct, 0)
        buf[chip, core] = ref[...]

    push(*pairs[0])

    for c in range(kv_local):
        for g in range(GROUP):
            h = c * GROUP + g
            qs[c, g * count:(g + 1) * count, :] = q_ref[:, h * HEAD_DIM:(h + 1) * HEAD_DIM]

    tile = 640 if features % 640 == 0 else HEAD_DIM

    def project(rows, t, first):
        for n in range(0, features, tile):
            here = dot(rows, wbuf[t, n:n + tile, :], NT)
            if first:
                acc[:, n:n + tile] = here
            else:
                acc[:, n:n + tile] = acc[:, n:n + tile] + here

    key_rows = 2 * count
    columns = GROUP * count
    query_pos = me * count + lax.broadcasted_iota(jnp.int32, (1, count), 1)
    query_start, _ = segment_facts(seq_ref, prompt_ref, query_pos)
    mass[...] = jnp.zeros(mass.shape, jnp.float32)
    factor = SCALE * math.log2(math.e)

    def rows_of(buf, p, c):
        return buf[p, :, :, c * HEAD_DIM:(c + 1) * HEAD_DIM].reshape(key_rows, HEAD_DIM)

    def score_step(step):
        p = chip - step

        if not (isinstance(step, int) and step == 0):
            arrived(k_ref, kbuf, k_recv, p, core)
            to_sibling(kbuf.at[p, core], kbuf, k_fwd, k_recv, p).start()

        arrived(k_ref, kbuf, k_recv, p, other)
        key_pos = (base + 2 * p) * count + lax.broadcasted_iota(jnp.int32, (key_rows, count), 0)
        allowed = (key_pos <= query_pos) & (key_pos >= query_start)
        bias = jnp.where(allowed, 0.0, NEG_LARGE).astype(jnp.float32)
        bias = jnp.concatenate([bias] * GROUP, axis=1)
        for c in range(kv_local):
            scores = dot(rows_of(kbuf, p, c), qs[c], NT) + bias
            before = top_ref[c]
            top = jnp.maximum(before, jnp.max(scores, axis=0, keepdims=True))
            shrink = jnp.exp2((before - top) * factor)
            weights = jnp.exp2((scores - top) * factor)
            probs[c, p] = weights
            peaks[c, p] = top
            mass[c] = mass[c] * shrink + jnp.sum(weights, axis=0, keepdims=True)
            top_ref[c] = top

    top_ref[...] = jnp.full(top_ref.shape, 4.0 * NEG_LARGE, jnp.float32)
    score_step(0)
    push(*pairs[1])

    w_copy(0).wait()
    project(og_ref[:, :chunk], 0, True)

    def own_step(t, carry):
        w_copy(t).wait()
        project(og_ref[:, pl.ds(pl.multiple_of(t * chunk, chunk), chunk)], t, False)
        return carry

    lax.fori_loop(1, chunks, own_step, 0)

    def far_step(t, carry):
        o = t // chunks
        ch = t % chunks
        w_copy(t).wait()
        og_copy(o, ch).wait_recv()
        project(ogbuf[o - 1, ch], t, False)
        return carry

    far = (nhead - 1) * chunks - 1

    def mixed_step(step, carry):
        @pl.when(step <= chip)
        def _():
            score_step(step)

        lax.fori_loop(
            chunks + far * (step - 1) // (chips - 1), chunks + far * step // (chips - 1),
            far_step, 0,
        )
        return carry

    lax.fori_loop(1, chips, mixed_step, 0)

    for c in range(kv_local):
        inverse = 1.0 / mass[c]

        def scale_step(p, carry, c=c, inverse=inverse):
            peaks[c, p] = jnp.exp2((peaks[c, p] - top_ref[c]) * factor) * inverse
            return carry

        lax.fori_loop(0, chip + 1, scale_step, 0)
    def value_step(step, carry):
        p = chip - step
        arrived(v_ref, vbuf, v_recv, p, core)
        to_sibling(vbuf.at[p, core], vbuf, v_fwd, v_recv, p).start()
        return carry

    lax.fori_loop(1, chip + 1, value_step, 0)

    far_step(chunks + far, 0)

    row_pos = me * count + lax.broadcasted_iota(jnp.int32, (count, HEAD_DIM), 0)
    _, answer_first = segment_facts(seq_ref, prompt_ref, row_pos)
    answer = (row_pos >= answer_first).astype(jnp.float32)
    for c in range(kv_local):
        for g in range(GROUP):
            h = c * GROUP + g
            gs[c, g * count:(g + 1) * count, :] = (
                acc[:, h * HEAD_DIM:(h + 1) * HEAD_DIM] * answer
            ).astype(jnp.bfloat16)

    def sib_copy(c, p):
        return remote(
            part.at[c, p, other], sib.at[c, p], sib_send.at[c, p], sib_recv.at[c, p], sibling, head
        )

    def ret_copy(c, p):
        return remote(
            sums.at[c, p], ret.at[c, chip], ret_send.at[c, p], ret_recv.at[c, chip],
            same_core(p), head,
        )

    def combine(c, p):
        sib_copy(c, p).wait_recv()
        sums[c, p] = (
            part[c, p, core].astype(jnp.float32) + sib[c, p].astype(jnp.float32)
        ).astype(jnp.bfloat16)
        ret_copy(c, p).start()

    together = 2 if kv_local % 2 == 0 else 1
    for start in range(0, kv_local, together):
        heads = range(start, start + together)
        for c in heads:
            dqt[c - start] = jnp.zeros(dqt.shape[1:], jnp.float32)

        def delta_step(p, deltas, heads=heads, start=start):
            if start == 0:
                arrived(v_ref, vbuf, v_recv, p, other)
            found = []
            for c in heads:
                here = dot(rows_of(vbuf, p, c), gs[c], NT)
                dprobs[c - start, p] = here
                found.append(
                    deltas[c - start]
                    + jnp.sum(probs[c, p] * here, axis=0, keepdims=True) * peaks[c, p]
                )
            return tuple(found)

        deltas = lax.fori_loop(
            0, chip + 1, delta_step, (jnp.zeros((1, columns), jnp.float32),) * together
        )

        def grad_step(p, carry, heads=heads, deltas=deltas, start=start):
            for c in heads:
                weights = probs[c, p] * peaks[c, p]
                dvalue = dot(weights.astype(jnp.bfloat16), gs[c], NN)
                dscores = (weights * (dprobs[c - start, p] - deltas[c - start])).astype(jnp.bfloat16)
                dkey = dot(dscores, qs[c], NN) * SCALE
                dqt[c - start] = dqt[c - start] + dot(rows_of(kbuf, p, c), dscores, TN)
                part[c, p, :, 0] = dkey.astype(jnp.bfloat16).reshape(2, count, HEAD_DIM)
                part[c, p, :, 1] = dvalue.astype(jnp.bfloat16).reshape(2, count, HEAD_DIM)
                sib_copy(c, p).start()

            @pl.when(p > 0)
            def _():
                for c in heads:
                    combine(c, p - 1)

            return carry

        lax.fori_loop(0, chip + 1, grad_step, 0)
        for c in heads:
            for g in range(GROUP):
                h = c * GROUP + g
                dq_ref[:, h * HEAD_DIM:(h + 1) * HEAD_DIM] = (
                    dqt[c - start, :, g * count:(g + 1) * count].T * SCALE
                ).astype(jnp.bfloat16)

    for c in range(kv_local):
        sib_copy(c, chip).wait_recv()
        total[c] = part[c, chip, core].astype(jnp.float32) + sib[c, chip].astype(jnp.float32)

    for c in range(kv_local):
        def collect(p, carry, c=c):
            pltpu.make_async_copy(sums.at[c, 0], ret.at[c, p], ret_recv.at[c, p]).wait()
            total[c] = total[c] + ret[c, p].astype(jnp.float32)
            return carry

        lax.fori_loop(chip + 1, chips, collect, 0)
        dk_ref[:, c * HEAD_DIM:(c + 1) * HEAD_DIM] = total[c, 0].astype(jnp.bfloat16)
        dv_ref[:, c * HEAD_DIM:(c + 1) * HEAD_DIM] = total[c, 1].astype(jnp.bfloat16)

    for ch in range(chunks):
        for o in range(1, nhead):
            og_copy(o, ch).wait_send()
    for ref, buf, send, recv, fwd in pairs:
        def sent_direct(p, carry, ref=ref, buf=buf, send=send, recv=recv):
            direct(ref, buf, send, recv, p).wait_send()
            return carry

        lax.fori_loop(chip + 1, chips, sent_direct, 0)

        def sent_on(p, carry, ref=ref, buf=buf, fwd=fwd, recv=recv):
            to_sibling(ref, buf, fwd, recv, p).wait_send()
            return carry

        lax.fori_loop(0, chip + 1, sent_on, 0)
    for c in range(kv_local):
        def sent_part(p, carry, c=c):
            sib_copy(c, p).wait_send()
            return carry

        lax.fori_loop(0, chip + 1, sent_part, 0)

        def sent_sum(p, carry, c=c):
            ret_copy(c, p).wait_send()
            return carry

        lax.fori_loop(0, chip, sent_sum, 0)


def hand_on(*refs):
    sources, targets, held = refs[:3], refs[3:6], refs[6:9]
    sem = refs[9]
    loads = [pltpu.make_async_copy(sources[i], held[i], sem.at[i]) for i in range(3)]
    stores = [pltpu.make_async_copy(held[i], targets[i], sem.at[3 + i]) for i in range(3)]
    for load in loads:
        load.start()
    for load, store in zip(loads, stores):
        load.wait()
        store.start()
    for store in stores:
        store.wait()


def shards(queries, keys, values, out_grad, out_weight, seq_lengths, prompt_lengths):
    nctx = lax.axis_size("ctx")
    nhead = lax.axis_size("head")
    count = queries.shape[0]
    kv_local = keys.shape[1] // HEAD_DIM
    chips = nctx // 4
    features = out_weight.shape[0]
    width = out_grad.shape[1]
    chunk = 512 if width % 512 == 0 else 256
    chunks = width // chunk
    columns = GROUP * count
    bf16, f32 = jnp.bfloat16, jnp.float32
    vmem = pl.BlockSpec(memory_space=pltpu.VMEM)
    smem = pl.BlockSpec(memory_space=pltpu.SMEM)
    dma = pltpu.SemaphoreType.DMA
    far = max(nhead - 1, 1)
    results = pl.pallas_call(
        functools.partial(kernel, nctx, nhead, chunk),
        out_shape=(
            jax.ShapeDtypeStruct(queries.shape, bf16),
            jax.ShapeDtypeStruct(keys.shape, bf16),
            jax.ShapeDtypeStruct(values.shape, bf16),
        ),
        in_specs=[vmem, vmem, vmem, vmem, pl.BlockSpec(memory_space=pl.ANY), smem, smem],
        out_specs=(vmem, vmem, vmem),
        scratch_shapes=[
            pltpu.VMEM((nhead * chunks, features, chunk), bf16),
            pltpu.VMEM((far, chunks, count, chunk), bf16),
            pltpu.VMEM((count, features), f32),
            pltpu.VMEM((kv_local, columns, HEAD_DIM), bf16),
            pltpu.VMEM((kv_local, columns, HEAD_DIM), bf16),
            pltpu.VMEM((chips, 2, count, kv_local * HEAD_DIM), bf16),
            pltpu.VMEM((chips, 2, count, kv_local * HEAD_DIM), bf16),
            pltpu.VMEM((kv_local, chips, 2 * count, columns), f32),
            pltpu.VMEM((kv_local, chips, 1, columns), f32),
            pltpu.VMEM((kv_local, 1, columns), f32),
            pltpu.VMEM((kv_local, 1, columns), f32),
            pltpu.VMEM((2, chips, 2 * count, columns), f32),
            pltpu.VMEM((2, HEAD_DIM, columns), f32),
            pltpu.VMEM((kv_local, chips, 2, 2, count, HEAD_DIM), bf16),
            pltpu.VMEM((kv_local, chips, 2, count, HEAD_DIM), bf16),
            pltpu.VMEM((kv_local, 2, count, HEAD_DIM), f32),
            pltpu.VMEM((kv_local, chips, 2, count, HEAD_DIM), bf16),
            pltpu.VMEM((kv_local, chips, 2, count, HEAD_DIM), bf16),
            dma((nhead * chunks,)),
            dma((far, chunks)),
            dma((far, chunks)),
            dma((chips,)),
            dma((chips,)),
            dma((chips, 2)),
            dma((chips, 2)),
            dma((chips,)),
            dma((chips,)),
            dma((kv_local, chips)),
            dma((kv_local, chips)),
            dma((kv_local, chips)),
            dma((kv_local, chips)),
        ],
        compiler_params=pltpu.CompilerParams(
            collective_id=0, has_side_effects=True, vmem_limit_bytes=60 * 1024 * 1024
        ),
    )(queries, keys, values, out_grad, out_weight, seq_lengths, prompt_lengths)
    anywhere = pl.BlockSpec(memory_space=pl.ANY)
    return pl.pallas_call(
        hand_on,
        out_shape=tuple(jax.ShapeDtypeStruct(r.shape, r.dtype) for r in results),
        in_specs=[anywhere] * 3,
        out_specs=(anywhere,) * 3,
        scratch_shapes=[pltpu.VMEM(r.shape, r.dtype) for r in results] + [dma((6,))],
        compiler_params=pltpu.CompilerParams(vmem_limit_bytes=60 * 1024 * 1024),
    )(*results)


def solution(mesh):
    return jax.shard_map(
        shards,
        mesh=mesh,
        in_specs=(
            P("ctx", "head"),
            P("ctx", "head"),
            P("ctx", "head"),
            P("ctx", "head"),
            P("head", None),
            P(),
            P(),
        ),
        out_specs=(P("ctx", "head"), P("ctx", "head"), P("ctx", "head")),
        check_vma=False,
    )
```

profile of v0, /device:TPU:5, one launch (start us, length us, event | category | flops | bytes accessed | tf_op | source)
XLA Modules:
  0.0 43.7 jit_solution(7882100328972280523)
XLA Ops:
  0.6 41.0 %shard_map.94 = (bf16[128,2560]{1,0:T(8,128)(2,1)}, bf16[128,512]{1,0:T(8,128)(2,1)}, bf16[128,512]{1,0:T(8,128)(2,1)}) custom-call(bf16[128,2560]{1,0:T(8,128)(2,1)} %q_ref.1, bf16[128,512]{1,0:T(8,128)(2,1)} %k_ref.1, bf16[128,512]{1,0:T(8,128)(2,1)} %v_ref.1, bf16[128,2560]{1,0:T(8,128)(2,1)} %og_ref.1, bf16[2560,5120]{1,0:T(8,128)(2,1)} %w_ref.1, ...), custom_call_target="tpu_custom_call" | custom-call | tf_op jit(solution)/shard_map/pallas_call | solution.py:379
  41.7 2.1 %shard_map.95 = (bf16[128,2560]{1,0:T(8,128)(2,1)}, bf16[128,512]{1,0:T(8,128)(2,1)}, bf16[128,512]{1,0:T(8,128)(2,1)}) custom-call(bf16[128,2560]{1,0:T(8,128)(2,1)} %get-tuple-element.6.refs_0_, bf16[128,512]{1,0:T(8,128)(2,1)} %get-tuple-element.7.refs_1_, bf16[128,512]{1,0:T(8,128)(2,1)} %get-tuple-element.8.refs_2_), custom_call_target="tpu_custom_call" | custom-call | tf_op jit(solution)/shard_map/pallas_call | solution.py:426
where the time goes:
time: 43.9 us; the launch traced here: 43.7 us
  Pallas kernels  43.1 us (98%)
  between operations  0.64 us (1%)
    pallas_call x1, Pallas kernels, shards(): pl.pallas_call(functools.partial(kernel, nctx, nhead, chunk), out_shape=(...  41 us
    pallas_call x1, Pallas kernels, shards(): pl.pallas_call(hand_on, out_shape=tuple((jax.ShapeDtypeStruct(r.shape, r....  2.05 us

commit v1 on v0

--- a/solution.py
+++ b/solution.py
@@ -40,8 +40,8 @@
     nctx, nhead, chunk,
     q_ref, k_ref, v_ref, og_ref, w_ref, seq_ref, prompt_ref,
     dq_ref, dk_ref, dv_ref,
-    wbuf, ogbuf, acc, qs, gs, kbuf, vbuf, probs, peaks, top_ref, mass, dprobs, dqt, part, sib, total, sums, ret,
-    w_sem, og_send, og_recv, k_send, v_send, k_recv, v_recv, k_fwd, v_fwd,
+    ogown, dqv, wbuf, ogbuf, acc, qs, gs, kbuf, vbuf, probs, peaks, top_ref, mass, dprobs, dqt, part, sib, total, sums, ret,
+    og_sem, q_sem, dq_sem, w_sem, og_send, og_recv, k_send, v_send, k_recv, v_recv, k_fwd, v_fwd,
     sib_send, sib_recv, ret_send, ret_recv,
 ):
     count = q_ref.shape[0]
@@ -74,7 +74,25 @@
             w_ref.at[:, pl.ds(pl.multiple_of(column, 128), chunk)], wbuf.at[t], w_sem.at[t]
         )
 
-    for t in range(nhead * chunks):
+    og_local = pltpu.make_async_copy(og_ref, ogown, og_sem)
+    k_local = pltpu.make_async_copy(k_ref, kbuf.at[chip, core], k_recv.at[chip, core])
+    v_local = pltpu.make_async_copy(v_ref, vbuf.at[chip, core], v_recv.at[chip, core])
+
+    def q_copy(c, g):
+        h = c * GROUP + g
+        return pltpu.make_async_copy(
+            q_ref.at[:, pl.ds(h * HEAD_DIM, HEAD_DIM)],
+            qs.at[c, pl.ds(g * count, count)], q_sem.at[c, g],
+        )
+
+    all_heads = [(c, g) for c in range(kv_local) for g in range(GROUP)]
+    k_local.start()
+    for c, g in all_heads:
+        q_copy(c, g).start()
+    og_local.start()
+    v_local.start()
+    early = 2
+    for t in range(early):
         w_copy(t).start()
 
     barrier = pltpu.get_barrier_semaphore()
@@ -119,14 +137,13 @@
             return carry
 
         lax.fori_loop(chip + 1, chips, send_direct, 0)
-        buf[chip, core] = ref[...]
 
     push(*pairs[0])
-
-    for c in range(kv_local):
-        for g in range(GROUP):
-            h = c * GROUP + g
-            qs[c, g * count:(g + 1) * count, :] = q_ref[:, h * HEAD_DIM:(h + 1) * HEAD_DIM]
+    for t in range(early, nhead * chunks):
+        w_copy(t).start()
+    for c, g in all_heads:
+        q_copy(c, g).wait()
+    k_local.wait()
 
     tile = 640 if features % 640 == 0 else HEAD_DIM
 
@@ -176,11 +193,12 @@
     push(*pairs[1])
 
     w_copy(0).wait()
-    project(og_ref[:, :chunk], 0, True)
+    og_local.wait()
+    project(ogown[:, :chunk], 0, True)
 
     def own_step(t, carry):
         w_copy(t).wait()
-        project(og_ref[:, pl.ds(pl.multiple_of(t * chunk, chunk), chunk)], t, False)
+        project(ogown[:, pl.ds(pl.multiple_of(t * chunk, chunk), chunk)], t, False)
         return carry
 
     lax.fori_loop(1, chunks, own_step, 0)
@@ -216,6 +234,8 @@
             return carry
 
         lax.fori_loop(0, chip + 1, scale_step, 0)
+    v_local.wait()
+
     def value_step(step, carry):
         p = chip - step
         arrived(v_ref, vbuf, v_recv, p, core)
@@ -253,6 +273,12 @@
             part[c, p, core].astype(jnp.float32) + sib[c, p].astype(jnp.float32)
         ).astype(jnp.bfloat16)
         ret_copy(c, p).start()
+
+    def dq_copy(start):
+        lanes = pl.ds(start * GROUP * HEAD_DIM, together * GROUP * HEAD_DIM)
+        return pltpu.make_async_copy(
+            dqv.at[:, lanes], dq_ref.at[:, lanes], dq_sem.at[start // together]
+        )
 
     together = 2 if kv_local % 2 == 0 else 1
     for start in range(0, kv_local, together):
@@ -299,9 +325,10 @@
         for c in heads:
             for g in range(GROUP):
                 h = c * GROUP + g
-                dq_ref[:, h * HEAD_DIM:(h + 1) * HEAD_DIM] = (
+                dqv[:, h * HEAD_DIM:(h + 1) * HEAD_DIM] = (
                     dqt[c - start, :, g * count:(g + 1) * count].T * SCALE
                 ).astype(jnp.bfloat16)
+        dq_copy(start).start()
 
     for c in range(kv_local):
         sib_copy(c, chip).wait_recv()
@@ -317,6 +344,8 @@
         dk_ref[:, c * HEAD_DIM:(c + 1) * HEAD_DIM] = total[c, 0].astype(jnp.bfloat16)
         dv_ref[:, c * HEAD_DIM:(c + 1) * HEAD_DIM] = total[c, 1].astype(jnp.bfloat16)
 
+    for start in range(0, kv_local, together):
+        dq_copy(start).wait()
     for ch in range(chunks):
         for o in range(1, nhead):
             og_copy(o, ch).wait_send()
@@ -383,9 +412,11 @@
             jax.ShapeDtypeStruct(keys.shape, bf16),
             jax.ShapeDtypeStruct(values.shape, bf16),
         ),
-        in_specs=[vmem, vmem, vmem, vmem, pl.BlockSpec(memory_space=pl.ANY), smem, smem],
-        out_specs=(vmem, vmem, vmem),
+        in_specs=[pl.BlockSpec(memory_space=pl.ANY)] * 5 + [smem, smem],
+        out_specs=(pl.BlockSpec(memory_space=pl.ANY), vmem, vmem),
         scratch_shapes=[
+            pltpu.VMEM(out_grad.shape, bf16),
+            pltpu.VMEM(queries.shape, bf16),
             pltpu.VMEM((nhead * chunks, features, chunk), bf16),
             pltpu.VMEM((far, chunks, count, chunk), bf16),
             pltpu.VMEM((count, features), f32),
@@ -404,6 +435,9 @@
             pltpu.VMEM((kv_local, 2, count, HEAD_DIM), f32),
             pltpu.VMEM((kv_local, chips, 2, count, HEAD_DIM), bf16),
             pltpu.VMEM((kv_local, chips, 2, count, HEAD_DIM), bf16),
+            dma(()),
+            dma((kv_local, GROUP)),
+            dma((kv_local,)),
             dma((nhead * chunks,)),
             dma((far, chunks)),
             dma((far, chunks)),

time: 43.9 us -> 43.4 us (0.989)
  Pallas kernels: 43.1 us -> 42.6 us
    pallas_call x1, Pallas kernels: 41 us -> 40.5 us  [shards(): pl.pallas_call(functools.partial(kernel, nctx, nhead, chunk), out_shape=(...]
where the time goes in v1:
time: 43.4 us; the launch traced here: 43.2 us
  Pallas kernels  42.6 us (98%)
  between operations  0.64 us (1%)
    pallas_call x1, Pallas kernels, shards(): pl.pallas_call(functools.partial(kernel, nctx, nhead, chunk), out_shape=(...  40.5 us
    pallas_call x1, Pallas kernels, shards(): pl.pallas_call(hand_on, out_shape=tuple((jax.ShapeDtypeStruct(r.shape, r....  2.05 us

profile of v1, /device:TPU:5, one launch (start us, length us, event | category | flops | bytes accessed | tf_op | source)
XLA Modules:
  0.0 43.2 jit_solution(2141773902713112348)
XLA Ops:
  0.6 40.5 %shard_map.94 = (bf16[128,2560]{1,0:T(8,128)(2,1)}, bf16[128,512]{1,0:T(8,128)(2,1)}, bf16[128,512]{1,0:T(8,128)(2,1)}) custom-call(bf16[128,2560]{1,0:T(8,128)(2,1)} %q_ref.1, bf16[128,512]{1,0:T(8,128)(2,1)} %k_ref.1, bf16[128,512]{1,0:T(8,128)(2,1)} %v_ref.1, bf16[128,2560]{1,0:T(8,128)(2,1)} %og_ref.1, bf16[2560,5120]{1,0:T(8,128)(2,1)} %w_ref.1, ...), custom_call_target="tpu_custom_call" | custom-call | tf_op jit(solution)/shard_map/pallas_call | solution.py:408
  41.2 2.1 %shard_map.95 = (bf16[128,2560]{1,0:T(8,128)(2,1)}, bf16[128,512]{1,0:T(8,128)(2,1)}, bf16[128,512]{1,0:T(8,128)(2,1)}) custom-call(bf16[128,2560]{1,0:T(8,128)(2,1)} %get-tuple-element.6.refs_0_, bf16[128,512]{1,0:T(8,128)(2,1)} %get-tuple-element.7.refs_1_, bf16[128,512]{1,0:T(8,128)(2,1)} %get-tuple-element.8.refs_2_), custom_call_target="tpu_custom_call" | custom-call | tf_op jit(solution)/shard_map/pallas_call | solution.py:460

commit v2 on v1

--- a/solution.py
+++ b/solution.py
@@ -313,11 +313,12 @@
                 part[c, p, :, 0] = dkey.astype(jnp.bfloat16).reshape(2, count, HEAD_DIM)
                 part[c, p, :, 1] = dvalue.astype(jnp.bfloat16).reshape(2, count, HEAD_DIM)
                 sib_copy(c, p).start()
-
-            @pl.when(p > 0)
-            def _():
-                for c in heads:
-                    combine(c, p - 1)
+                if c == start:
+                    @pl.when(p > 0)
+                    def _():
+                        for earlier in heads:
+                            combine(earlier, p - 1)
+
 
             return carry
 

time: 43.4 us -> 44.2 us (1.018)
  Pallas kernels: 42.6 us -> 43.4 us
    pallas_call x1, Pallas kernels: 40.5 us -> 41.3 us  [shards(): pl.pallas_call(functools.partial(kernel, nctx, nhead, chunk), out_shape=(...]
where the time goes in v2:
time: 44.2 us; the launch traced here: 44 us
  Pallas kernels  43.4 us (98%)
  between operations  0.64 us (1%)
    pallas_call x1, Pallas kernels, shards(): pl.pallas_call(functools.partial(kernel, nctx, nhead, chunk), out_shape=(...  41.3 us
    pallas_call x1, Pallas kernels, shards(): pl.pallas_call(hand_on, out_shape=tuple((jax.ShapeDtypeStruct(r.shape, r....  2.05 us

profile of v2, /device:TPU:5, one launch (start us, length us, event | category | flops | bytes accessed | tf_op | source)
XLA Modules:
  0.0 44.0 jit_solution(16630294654303177138)
XLA Ops:
  0.6 41.3 %shard_map.94 = (bf16[128,2560]{1,0:T(8,128)(2,1)}, bf16[128,512]{1,0:T(8,128)(2,1)}, bf16[128,512]{1,0:T(8,128)(2,1)}) custom-call(bf16[128,2560]{1,0:T(8,128)(2,1)} %q_ref.1, bf16[128,512]{1,0:T(8,128)(2,1)} %k_ref.1, bf16[128,512]{1,0:T(8,128)(2,1)} %v_ref.1, bf16[128,2560]{1,0:T(8,128)(2,1)} %og_ref.1, bf16[2560,5120]{1,0:T(8,128)(2,1)} %w_ref.1, ...), custom_call_target="tpu_custom_call" | custom-call | tf_op jit(solution)/shard_map/pallas_call | solution.py:409
  41.9 2.1 %shard_map.95 = (bf16[128,2560]{1,0:T(8,128)(2,1)}, bf16[128,512]{1,0:T(8,128)(2,1)}, bf16[128,512]{1,0:T(8,128)(2,1)}) custom-call(bf16[128,2560]{1,0:T(8,128)(2,1)} %get-tuple-element.6.refs_0_, bf16[128,512]{1,0:T(8,128)(2,1)} %get-tuple-element.7.refs_1_, bf16[128,512]{1,0:T(8,128)(2,1)} %get-tuple-element.8.refs_2_), custom_call_target="tpu_custom_call" | custom-call | tf_op jit(solution)/shard_map/pallas_call | solution.py:461
